TPU v7x, 32 devices: a whole 2x2x4 slice. The times are simulated.
32 devices in a mesh: rows: 16 (over z, y, core), cols: 2 (over x).
Axes of the slice: x: 2, y: 2, z: 4, core: 2. Of those that a mesh axis runs over, the one named last changes fastest.
Arguments:
- vectors: float32 [128, 32768], P(None, ('rows', 'cols')), may hold values from -80 to 80
- offsets: int32 [16, 32768], P(None, ('rows', 'cols')), may hold values from -256 to 256, as said below
- counts: int32 [32768], P(('rows', 'cols')), may hold values from 8 to 16
- labels: int32 [2, 32768], P(None, ('rows', 'cols')), may hold values from 0 to 1
- cosines: float32 [16, 32768], P(None, ('rows', 'cols')), may hold values from -1 to 1
- distances: float32 [16, 32768], P(None, ('rows', 'cols')), may hold values from 1 to 3
Outputs:
- basis: float32 [128, 32768], P('cols', 'rows')
Inputs may be any that keep to these rules, and one draw needn't show every extreme that they name: `offsets`: each offset is nonzero and at most 256 in magnitude; both -256 and 256 occur. Offsets follow a lattice: small in-row steps, steps near half of 256, and steps near 256.
All inputs are finite; a program needn't handle non-finite values.
Results may differ from a plain program's by a relative error of at most 0.00012.
Values sent between devices are 32-bit elements; how exact they have to be, the bound alone decides.
A program may use at most 64 MiB of HBM per device.

v0:
```python
import jax
import jax.numpy as jnp
from jax import lax
from jax.sharding import PartitionSpec as P

REACH = 256


PI_BOND = -1.0
SIGMA_BOND = 0.178
DECAY_LENGTH = 0.319
LAYER_GAP = 2.36
SITE_MASS = 0.4
LAYER_BIAS = 0.25


def extended_2(block, sides, width):
    for axis, dim in sides:
        count = lax.axis_size(axis)
        forward = [(i, i + 1) for i in range(count - 1)]
        forward.append((count - 1, 0))
        backward = [(target, source) for source, target in forward]
        low = lax.ppermute(
            lax.slice_in_dim(block, block.shape[dim] - width, None, axis=dim), axis, forward
        )
        high = lax.ppermute(lax.slice_in_dim(block, 0, width, axis=dim), axis, backward)
        block = jnp.concatenate([low, block, high], axis=dim)
    return block


def spread(value, axis, source):
    kept = jnp.where(lax.axis_index(axis) == source, value, 0).astype(value.dtype)
    return lax.psum(kept, axis)


def hop_table(cosines, distances, counts):
    square = cosines * cosines
    bond_value = PI_BOND * jnp.exp(-(distances - 1.0) / DECAY_LENGTH) * (1.0 - square)
    bond_value = bond_value + SIGMA_BOND * jnp.exp(-(distances - LAYER_GAP) / DECAY_LENGTH) * square
    slot_index = lax.broadcasted_iota(jnp.int32, cosines.shape, 0)
    return jnp.where(slot_index < counts[None, :], bond_value, jnp.zeros_like(bond_value))


def onsite_of(labels):
    sublattice = (2 * labels[0] - 1).astype(jnp.float32)
    layer_sign = (2 * labels[1] - 1).astype(jnp.float32)
    return SITE_MASS * sublattice + LAYER_BIAS * layer_sign


def apply_local(extended, hopping, offsets, onsite):
    atom_count = hopping.shape[1]
    middle = extended[:, REACH : REACH + atom_count]
    column = jnp.arange(atom_count, dtype=jnp.int32) + REACH

    def advance(slot_index, running):
        target = column + offsets[slot_index]
        return running + hopping[slot_index][None, :] * jnp.take(extended, target, axis=1)

    return lax.fori_loop(0, hopping.shape[0], advance, onsite[None, :] * middle)


def regroup(source):
    return lax.all_to_all(source, "cols", split_axis=0, concat_axis=1, tiled=True)


def on_device(vectors, offsets, counts, labels, cosines, distances):
    highest = lax.Precision.HIGHEST
    hopping = hop_table(cosines, distances, counts)
    onsite = onsite_of(labels)
    applied = vectors
    for repeat in range(2):
        extended = extended_2(applied, ((("rows", "cols"), 1),), REACH)
        applied = apply_local(extended, hopping, offsets, onsite)
    local_block = regroup(applied)
    atom_total = local_block.shape[1] * lax.axis_size("rows")
    step_count = min(3, lax.axis_size("cols") - 1)
    column_index = lax.axis_index("cols")
    for step_index in range(step_count):
        gram_matrix = (
            lax.psum(jnp.dot(local_block, local_block.T, precision=highest), "rows") / atom_total
        )
        factor = jnp.linalg.cholesky(gram_matrix)
        candidate = jax.scipy.linalg.solve_triangular(factor, local_block, lower=True)
        leader = spread(candidate, "cols", step_index)
        coupling = lax.psum(jnp.dot(leader, local_block.T, precision=highest), "rows") / atom_total
        reduced = local_block - jnp.dot(coupling.T, leader, precision=highest)
        local_block = jnp.where(
            column_index > step_index,
            reduced,
            jnp.where(column_index == step_index, leader, local_block),
        )
    return local_block


def solution(mesh):
    placed = (
        P(None, ("rows", "cols")),
        P(None, ("rows", "cols")),
        P(("rows", "cols")),
        P(None, ("rows", "cols")),
        P(None, ("rows", "cols")),
        P(None, ("rows", "cols")),
    )
    return jax.shard_map(
        on_device, mesh=mesh, in_specs=placed, out_specs=P("cols", "rows"), check_vma=False
    )
```

profile of v0, /device:TPU:0, one launch (start us, length us, event | category | flops | bytes accessed | tf_op | source)
XLA Modules:
  0.0 341.5 jit_solution(12983269690168434741)
XLA Ops:
  7.8 3.0 collective-permute-start
  10.8 3.5 %collective-permute-start.1 = (f32[128,256]{0,1:T(8,128)S(1)}, f32[128,256]{0,1:T(8,128)S(1)}, u32[]{:S(2)}, u32[]{:S(2)}) collective-permute-start(f32[128,256]{0,1:T(8,128)S(1)} %get-tuple-element.273), channel_id=1, source_target_pairs={{1,0},{2,1},{3,2},{4,3},{5,4},{6,5},{7,6},{8,7},{9,8},{10,9},{11,1... | collective-permute-start | bytes 393224 | tf_op jit(solution)/shard_map/ppermute | solution.py:26
  17.2 66.3 %while.28 = (s32[]{:T(128)}, f32[128,1024]{0,1:T(8,128)S(1)}, f32[16,1024]{1,0:T(8,128)S(1)}, s32[16,1024]{1,0:T(8,128)}, f32[128,1536]{0,1:T(8,128)S(1)}, /*index=5*/s32[]{:T(128)}) while((s32[]{:T(128)}, f32[128,1024]{0,1:T(8,128)S(1)}, f32[16,1024]{1,0:T(8,128)S(1)}, s32[16,1024]{1,0:T(8,128)}, f32[128,1536]{0,1:T(8,128)S(1)}, ...), condition=%wide.region_1.0_spmd.clone, body=%wide.region_0.2_spmd.clone.sunk | while | flops 407554 | bytes 2660429 | solution.py:59
  18.0 2.8 gather_fusion
  22.2 2.8 gather_fusion
  26.3 2.8 gather_fusion
  30.5 2.8 gather_fusion
  34.6 2.8 gather_fusion
  38.8 2.8 gather_fusion
  42.9 2.8 gather_fusion
  47.0 2.8 gather_fusion
  51.2 2.8 gather_fusion
  63.6 2.8 gather_fusion
  67.7 2.8 gather_fusion
  80.2 2.8 gather_fusion
  83.9 5.1 %collective-permute-start.3 = (f32[128,256]{0,1:T(8,128)S(1)}, f32[128,256]{0,1:T(8,128)S(1)}, u32[]{:S(2)}, u32[]{:S(2)}) collective-permute-start(f32[128,256]{0,1:T(8,128)S(1)} %get-tuple-element.271), channel_id=1, source_target_pairs={{1,0},{2,1},{3,2},{4,3},{5,4},{6,5},{7,6},{8,7},{9,8},{10,9},{11,1... | collective-permute-start | bytes 393224 | tf_op jit(solution)/shard_map/ppermute | solution.py:26
  92.1 66.3 %while.29 = (s32[]{:T(128)}, f32[128,1024]{0,1:T(8,128)S(1)}, f32[16,1024]{1,0:T(8,128)S(1)}, s32[16,1024]{1,0:T(8,128)}, f32[128,1536]{0,1:T(8,128)S(1)}, /*index=5*/s32[]{:T(128)}) while((s32[]{:T(128)}, f32[128,1024]{0,1:T(8,128)S(1)}, f32[16,1024]{1,0:T(8,128)S(1)}, s32[16,1024]{1,0:T(8,128)}, f32[128,1536]{0,1:T(8,128)S(1)}, ...), condition=%wide.region_3.5_spmd.clone, body=%wide.region_2.4_spmd.clone.sunk | while | flops 407554 | bytes 2660429 | solution.py:59
  97.0 2.8 gather_fusion.1
  101.2 2.8 gather_fusion.1
  113.6 2.8 gather_fusion.1
  117.8 2.8 gather_fusion.1
  130.2 2.8 gather_fusion.1
  134.3 2.8 gather_fusion.1
  146.8 2.8 gather_fusion.1
  150.9 2.8 gather_fusion.1
  159.4 3.5 %all-to-all-start = ((f32[2,64,1024]{2,1,0:T(8,128)}), f32[2,64,1024]{2,1,0:T(8,128)S(1)}, u32[]{:S(2)}, u32[]{:S(2)}) async-start(f32[2,64,1024]{2,1,0:T(8,128)} %bitcast.1), calls=%async_computation | async-start | bytes 1048576 | tf_op jit(solution)/shard_map/all_to_all | solution.py:63
  162.9 9.1 %all-to-all-done = f32[2,64,1024]{2,1,0:T(8,128)S(1)} async-done(((f32[2,64,1024]{2,1,0:T(8,128)}), f32[2,64,1024]{2,1,0:T(8,128)S(1)}, u32[]{:S(2)}, u32[]{:S(2)}) %all-to-all-start) | async-done | bytes 524320 | tf_op jit(solution)/shard_map/all_to_all | solution.py:63
  172.6 58.9 %psum.21 = f32[64,64]{0,1:T(8,128)S(1)} all-reduce(f32[64,64]{0,1:T(8,128)S(1)} %convolution_bitcast_fusion), channel_id=1, replica_groups=mesh['rows'=16,'cols'=2] {'rows'}, use_global_device_ids=true, to_apply=%region_4.6 | all-reduce | flops 4096 | bytes 32768 | tf_op jit(solution)/shard_map/psum | solution.py:80
  231.6 5.9 %cholesky.16 = f32[64,64]{1,0:T(8,128)S(1)} custom-call(f32[64,64]{1,0:T(8,128)S(1)} %fusion.12), custom_call_target="Cholesky" | custom-call | tf_op jit(solution)/shard_map/jit(cholesky)/cholesky | solution.py:82
  238.8 4.9 %custom-call.7 = f32[1,64,64]{1,2,0:T(8,128)S(1)} custom-call(f32[1,64,64]{2,1,0:T(8,128)S(1)} %fusion.10), custom_call_target="InvertDiagBlocksLowerTriangular" | custom-call | tf_op jit(solution)/shard_map/jit(_solve_triangular)/triangular_solve | solution.py:83
  245.2 25.1 %all-reduce.2.cloned.1.call-done = f32[64,2048]{1,0:T(8,128)} async-done(((f32[64,2048]{1,0:T(8,128)}), f32[64,2048]{1,0:T(8,128)}) %all-reduce.2.cloned.1.call-update) | async-done | bytes 524304 | tf_op jit(solution)/shard_map/psum | solution.py:33
  272.0 61.2 %psum.23 = f32[64,64]{0,1:T(8,128)S(1)} all-reduce(f32[64,64]{0,1:T(8,128)S(1)} %fusion.18), channel_id=1, replica_groups=mesh['rows'=16,'cols'=2] {'rows'}, use_global_device_ids=true, to_apply=%region_8.10 | all-reduce | flops 4096 | bytes 32768 | tf_op jit(solution)/shard_map/psum | solution.py:85
  (210 shorter events, 90.2 us)
Async XLA Ops:
  7.8 6.6 %copy-start.3 = (s32[2,1024]{1,0:T(2,128)S(1)}, s32[2,1024]{1,0:T(2,128)}, u32[]{:S(2)}) copy-start(s32[2,1024]{1,0:T(2,128)} %param.15) | copy-start | bytes 24580
  7.8 9.2 %collective-permute-start = (f32[128,256]{0,1:T(8,128)S(1)}, f32[128,256]{0,1:T(8,128)S(1)}, u32[]{:S(2)}, u32[]{:S(2)}) collective-permute-start(f32[128,256]{0,1:T(8,128)S(1)} %get-tuple-element.272), channel_id=1, source_target_pairs={{0,1},{1,2},{2,3},{3,4},{4,5},{5,6},{6,7},{7,8},{8,9},{9,10},{10,1... | collective-permute-start | bytes 393224 | tf_op jit(solution)/shard_map/ppermute | solution.py:23
  10.8 6.4 %collective-permute-start.1 = (f32[128,256]{0,1:T(8,128)S(1)}, f32[128,256]{0,1:T(8,128)S(1)}, u32[]{:S(2)}, u32[]{:S(2)}) collective-permute-start(f32[128,256]{0,1:T(8,128)S(1)} %get-tuple-element.273), channel_id=1, source_target_pairs={{1,0},{2,1},{3,2},{4,3},{5,4},{6,5},{7,6},{8,7},{9,8},{10,9},{11,1... | collective-permute-start | bytes 393224 | tf_op jit(solution)/shard_map/ppermute | solution.py:26
  14.3 0.8 copy-start.1
  14.4 0.9 copy-start.2
  14.4 0.9 copy-start.4
  83.6 8.2 %collective-permute-start.2 = (f32[128,256]{0,1:T(8,128)S(1)}, f32[128,256]{0,1:T(8,128)S(1)}, u32[]{:S(2)}, u32[]{:S(2)}) collective-permute-start(f32[128,256]{0,1:T(8,128)S(1)} %get-tuple-element.270), channel_id=1, source_target_pairs={{0,1},{1,2},{2,3},{3,4},{4,5},{5,6},{6,7},{7,8},{8,9},{9,10},{10,1... | collective-permute-start | bytes 393224 | tf_op jit(solution)/shard_map/ppermute | solution.py:23
  83.9 8.2 %collective-permute-start.3 = (f32[128,256]{0,1:T(8,128)S(1)}, f32[128,256]{0,1:T(8,128)S(1)}, u32[]{:S(2)}, u32[]{:S(2)}) collective-permute-start(f32[128,256]{0,1:T(8,128)S(1)} %get-tuple-element.271), channel_id=1, source_target_pairs={{1,0},{2,1},{3,2},{4,3},{5,4},{6,5},{7,6},{8,7},{9,8},{10,9},{11,1... | collective-permute-start | bytes 393224 | tf_op jit(solution)/shard_map/ppermute | solution.py:26
  159.4 12.7 %all-to-all-start = ((f32[2,64,1024]{2,1,0:T(8,128)}), f32[2,64,1024]{2,1,0:T(8,128)S(1)}, u32[]{:S(2)}, u32[]{:S(2)}) async-start(f32[2,64,1024]{2,1,0:T(8,128)} %bitcast.1), calls=%async_computation | async-start | bytes 1048576 | tf_op jit(solution)/shard_map/all_to_all | solution.py:63
  162.9 107.4 %all-reduce.2.cloned.1.call-start = ((), (), s32[]{:S(2)}) async-start(), calls=%async_computation.1 | async-start | bytes 1048576 | tf_op jit(solution)/shard_map/psum | solution.py:33
  270.3 62.9 %copy-start = (f32[64,2048]{1,0:T(8,128)S(1)}, f32[64,2048]{1,0:T(8,128)}, u32[]{:S(2)}) copy-start(f32[64,2048]{1,0:T(8,128)} %all-reduce.2.cloned.1.call-done) | copy-start | bytes 1572868
Sparse Core Ops, SparseCore 0:
  245.3 24.9 all-reduce.1
where the time goes:
time: 344 us; the launch traced here: 341 us
  blocking collectives  120 us (35%)
  local copies, waits for them, and re-layouts  118 us (34%)
  waiting for transfers between devices  39.1 us (11%)
  other arithmetic  29 us (8%)
  starting transfers between devices  15.4 us (4%)
  between operations  13.6 us (4%)
  matrix products  5.06 us (1%)
    gather x32, local copies, waits for them, and re-layouts, advance(): jnp.take(extended, target, axis=1)  89.8 us
    psum x1, blocking collectives, on_device(): lax.psum(jnp.dot(leader, local_block.T, precision=highest), 'rows')  61.2 us
    psum x1, blocking collectives, on_device(): lax.psum(jnp.dot(local_block, local_block.T, precision=highest), 'rows')  58.9 us
    psum x1, waiting for transfers between devices, spread(): return lax.psum(kept, axis)  25.1 us
    dynamic_slice x32, local copies, waits for them, and re-layouts, advance(): target = column + offsets[slot_index]  24.6 us
    add x32, other arithmetic, advance(): running + hopping[slot_index][None, :] * jnp.take(extended, target, axis=1)  15.7 us
    all_to_all x1, waiting for transfers between devices, regroup(): lax.all_to_all(source, 'cols', split_axis=0, concat_axis=1, tiled=True)  9.12 us
    ppermute x2, starting transfers between devices, extended_2(): lax.ppermute(lax.slice_in_dim(block, 0, width, axis=dim), axis, backward)  8.58 us
  transfers between devices with their start and end apart: 6, of which 6 were waited for; matrix products, arithmetic and copies ran while one was open for 0% of the time, Pallas kernels for 0%

commit v1 on v0

--- a/solution.py
+++ b/solution.py
@@ -1,6 +1,10 @@
+import functools
+
 import jax
 import jax.numpy as jnp
 from jax import lax
+from jax.experimental import pallas as pl
+from jax.experimental.pallas import tpu as pltpu
 from jax.sharding import PartitionSpec as P
 
 REACH = 256
@@ -92,6 +96,334 @@
     return local_block
 
 
+BLOCK = 64
+TILE = 256
+SPAN = TILE + 2 * REACH
+HALF = 128
+BAND = HALF + 2 * REACH
+MESH = pl.DeviceIdType.MESH
+
+
+def split_2(value):
+    high = value.astype(jnp.bfloat16)
+    low = (value - high.astype(jnp.float32)).astype(jnp.bfloat16)
+    return high, low
+
+
+def dot_nn(left, right):
+    return lax.dot_general(
+        left, right, (((1,), (0,)), ((), ())), preferred_element_type=jnp.float32
+    )
+
+
+def dot_nt(left, right):
+    return lax.dot_general(
+        left, right, (((1,), (1,)), ((), ())), preferred_element_type=jnp.float32
+    )
+
+
+def inverse_factor(gram):
+    size = gram.shape[0]
+    rows = lax.broadcasted_iota(jnp.int32, (size, size), 0)
+    lanes = lax.broadcasted_iota(jnp.int32, (size, size), 1)
+    eye = jnp.where(rows == lanes, 1.0, 0.0).astype(jnp.float32)
+    wide = jnp.concatenate([gram, eye], axis=1)
+    parts = [wide[8 * b : 8 * b + 8, :] for b in range(size // 8)]
+    sub = lax.broadcasted_iota(jnp.int32, (8, 1), 0)
+    for k in range(size - 1):
+        b, s = k // 8, k % 8
+        row = parts[b][s : s + 1, :]
+        scaled = row * (1.0 / row[:, k : k + 1])
+        for i in range(b, size // 8):
+            column = parts[i][:, k : k + 1]
+            if i == b:
+                column = jnp.where(sub > s, column, 0.0)
+            parts[i] = parts[i] - column * scaled
+    done = jnp.concatenate(parts, axis=0)
+    pivots = jnp.sum(jnp.where(rows == lanes, done[:, :size], 0.0), axis=1, keepdims=True)
+    return done[:, size:] / jnp.sqrt(pivots)
+
+
+def kernel(
+    row_count, col_count, atom_total,
+    v_ref, off_ref, cnt_ref, lab_ref, cos_ref, dist_ref, out_ref,
+    key, hop, site, w_high, w_low, ext, mid, fin, halo, gram, rs, slab, zs, tot, gat, swap,
+    send, recv,
+):
+    vector_count, local = v_ref.shape
+    tiles = local // TILE
+    planes = row_count // 4
+    r, c = lax.axis_index("rows"), lax.axis_index("cols")
+    place = r * col_count + c
+    total = row_count * col_count
+    ahead = lax.rem(place + 1, total)
+    behind = lax.rem(place + total - 1, total)
+    right = (ahead // col_count, lax.rem(ahead, col_count))
+    left = (behind // col_count, lax.rem(behind, col_count))
+    bit0, bit1 = lax.rem(r, 2), lax.rem(r // 2, 2)
+    z = r // 4
+    mine = c + 2 * lax.rem(r, 4)
+
+    group = []
+    for j in range(1, 8):
+        pc = 1 - c if j & 1 else c
+        p0 = 1 - bit0 if j & 2 else bit0
+        p1 = 1 - bit1 if j & 4 else bit1
+        group.append(((4 * z + 2 * p1 + p0, pc), pc + 2 * p0 + 4 * p1))
+    peers = [
+        (4 * lax.rem(z + d, planes) + lax.rem(r, 4), c) for d in range(1, planes)
+    ]
+
+    barrier = pltpu.get_barrier_semaphore()
+    greeted = [left, right] + [g[0] for g in group] + peers
+    for device in greeted:
+        pl.semaphore_signal(barrier, inc=1, device_id=device, device_id_type=MESH)
+    pl.semaphore_wait(barrier, len(greeted))
+
+    def remote(slot, source, target, device):
+        return pltpu.make_async_remote_copy(
+            src_ref=source, dst_ref=target, send_sem=send.at[slot], recv_sem=recv.at[slot],
+            device_id=device, device_id_type=MESH,
+        )
+
+    def edges(source, first):
+        low = source.at[:, pl.ds(local - REACH, REACH)]
+        high = source.at[:, pl.ds(0, REACH)]
+        to_right = remote(first, low, halo.at[first], right)
+        to_left = remote(first + 1, high, halo.at[first + 1], left)
+        to_right.start()
+        to_left.start()
+        return to_right, to_left
+
+    halo_a = edges(v_ref, 0)
+
+    lane = lax.broadcasted_iota(jnp.int32, (1, local), 1)
+    key[...] = off_ref[...] + (lax.rem(lane, HALF) + REACH)
+    hop[...] = hop_table_2(cos_ref[...], dist_ref[...], cnt_ref[...])
+    lab = lab_ref[...]
+    signs = (2 * lab - 1).astype(jnp.float32)
+    site[...] = SITE_MASS * signs[0:1, :] + LAYER_BIAS * signs[1:2, :]
+
+    def put_ext(value, first, width):
+        high, low = split_2(value)
+        ext[0:vector_count, first : first + width] = high
+        ext[vector_count : 2 * vector_count, first : first + width] = low
+
+    put_ext(v_ref[...], REACH, local)
+
+    slots = off_ref.shape[0]
+    chunk = 32
+    row8 = lax.broadcasted_iota(jnp.int32, (8, HALF), 0)
+
+    def build(t, carry):
+        for half in range(2):
+            lanes = pl.ds(pl.multiple_of(t * TILE + half * HALF, HALF), HALF)
+            keys = key[:, lanes]
+            hops = hop[:, lanes]
+            keys = [jnp.broadcast_to(keys[k : k + 1, :], (8, HALF)) for k in range(slots)]
+            hops = [jnp.broadcast_to(hops[k : k + 1, :], (8, HALF)) for k in range(slots)]
+
+            def rows(q, inner):
+                parts = []
+                for piece in range(chunk // 8):
+                    index = row8 + (q * chunk + piece * 8)
+                    terms = jnp.where(keys[0] == index, hops[0], 0.0)
+                    for k in range(1, slots):
+                        terms = terms + jnp.where(keys[k] == index, hops[k], 0.0)
+                    parts.append(terms)
+                high, low = split_2(jnp.concatenate(parts, axis=0))
+                where = pl.ds(pl.multiple_of(q * chunk + half * HALF, chunk), chunk)
+                span = pl.ds(half * HALF, HALF)
+                w_high[t, where, span] = high
+                w_low[t, where, span] = low
+                return inner
+
+            lax.fori_loop(0, BAND // chunk, rows, 0)
+            blank = jnp.zeros((HALF, HALF), jnp.bfloat16)
+            edge = pl.ds(BAND if half == 0 else 0, HALF)
+            w_high[t, edge, pl.ds(half * HALF, HALF)] = blank
+            w_low[t, edge, pl.ds(half * HALF, HALF)] = blank
+        return carry
+
+    lax.fori_loop(0, tiles, build, 0)
+
+    def apply(t, source, target):
+        lanes = slice(t * TILE, (t + 1) * TILE)
+        span = slice(t * TILE, t * TILE + SPAN)
+        both = dot_nn(ext[:, span], w_high[t])
+        value = both[0:vector_count] + both[vector_count:]
+        value = value + dot_nn(ext[0:vector_count, span], w_low[t])
+        target[:, lanes] = value + site[:, lanes] * source[:, lanes]
+
+    def finish(source, target, arrivals, first):
+        to_right, to_left = arrivals
+        for t in range(1, tiles - 1):
+            apply(t, source, target)
+        to_right.wait_recv()
+        put_ext(halo[first], 0, REACH)
+        apply(0, source, target)
+        to_left.wait_recv()
+        put_ext(halo[first + 1], REACH + local, REACH)
+        apply(tiles - 1, source, target)
+
+    finish(v_ref, mid, halo_a, 0)
+    halo_b = edges(mid, 2)
+    put_ext(mid[...], REACH, local)
+    finish(mid, fin, halo_b, 2)
+
+    high, low = split_2(fin[...])
+    lead = jnp.concatenate([high[0:BLOCK], low[0:BLOCK]], axis=0)
+    pair = dot_nt(lead, jnp.concatenate([high, low], axis=0))
+    part = pair[0:BLOCK, 0:vector_count] + (
+        pair[BLOCK:, 0:vector_count] + pair[0:BLOCK, vector_count:]
+    )
+    part = part * (1.0 / atom_total)
+    for b in range(8):
+        gram[b] = part[8 * b : 8 * b + 8, :]
+
+    first = 4
+    scatter = []
+    for j in range(7):
+        device, index = group[j]
+        copy = remote(first + j, gram.at[index], rs.at[j], device)
+        copy.start()
+        scatter.append(copy)
+
+    partner = (r, 1 - c)
+    swap_a = remote(28, fin.at[pl.ds(0, BLOCK)], swap.at[pl.ds(0, BLOCK)], partner)
+    swap_b = remote(29, fin.at[pl.ds(BLOCK, BLOCK)], swap.at[pl.ds(BLOCK, BLOCK)], partner)
+    swap_a.start()
+
+    @pl.when(c == 0)
+    def _():
+        swap_b.start()
+
+    value = gram[mine]
+    for j in range(7):
+        scatter[j].wait_recv()
+        value = value + rs[j]
+    slab[...] = value
+    across = []
+    for d in range(planes - 1):
+        copy = remote(11 + d, slab, zs.at[d], peers[d])
+        copy.start()
+        across.append(copy)
+    for d in range(planes - 1):
+        across[d].wait_recv()
+        value = value + zs[d]
+    tot[...] = value
+    gather = []
+    for j in range(7):
+        copy = remote(21 + j, tot, gat.at[mine], group[j][0])
+        copy.start()
+        gather.append(copy)
+    gat[mine] = value
+    for j in range(7):
+        gather[j].wait_recv()
+
+    highest = lax.Precision.HIGHEST
+    full = jnp.concatenate([gat[b] for b in range(8)], axis=0)
+    inverse = inverse_factor(full[:, 0:BLOCK])
+    coupling = jnp.dot(
+        inverse, full[:, BLOCK:], precision=highest, preferred_element_type=jnp.float32
+    )
+    update = lax.dot_general(
+        coupling, inverse, (((0,), (0,)), ((), ())), precision=highest,
+        preferred_element_type=jnp.float32,
+    )
+    owner = c == 0
+    factor_high, factor_low = split_2(jnp.where(owner, inverse, -update))
+    factor = jnp.concatenate([factor_high, factor_low], axis=0)
+
+    def result(lead_high, lead_low, own):
+        both = dot_nn(factor, lead_high)
+        value = both[0:BLOCK] + both[BLOCK:] + dot_nn(factor_high, lead_low)
+        return value + jnp.where(owner, 0.0, own)
+
+    own = result(high[0:BLOCK], low[0:BLOCK], fin[BLOCK:, :])
+    out_ref[:, pl.ds(pl.multiple_of(c * local, local), local)] = own
+
+    swap_a.wait_recv()
+
+    @pl.when(c == 1)
+    def _():
+        swap_b.wait_recv()
+
+    other_high, other_low = split_2(swap[0:BLOCK, :])
+    theirs = result(other_high, other_low, swap[BLOCK:, :])
+    out_ref[:, pl.ds(pl.multiple_of((1 - c) * local, local), local)] = theirs
+
+    for copy in (*halo_a, *halo_b, *scatter, *across, *gather, swap_a):
+        copy.wait_send()
+
+    @pl.when(c == 0)
+    def _():
+        swap_b.wait_send()
+
+
+def hop_table_2(cosines, distances, counts):
+    square = cosines * cosines
+    bond_value = PI_BOND * jnp.exp(-(distances - 1.0) / DECAY_LENGTH) * (1.0 - square)
+    bond_value = bond_value + SIGMA_BOND * jnp.exp(-(distances - LAYER_GAP) / DECAY_LENGTH) * square
+    slot_index = lax.broadcasted_iota(jnp.int32, cosines.shape, 0)
+    return jnp.where(slot_index < counts, bond_value, jnp.zeros_like(bond_value))
+
+
+def fused(row_count, col_count, vectors, offsets, counts, labels, cosines, distances):
+    vector_count, local = vectors.shape
+    slots = offsets.shape[0]
+    tiles = local // TILE
+    planes = row_count // 4
+    f32, bf16 = jnp.float32, jnp.bfloat16
+    vmem = pl.BlockSpec(memory_space=pltpu.VMEM)
+    return pl.pallas_call(
+        functools.partial(kernel, row_count, col_count, local * row_count * col_count),
+        out_shape=jax.ShapeDtypeStruct((BLOCK, local * col_count), f32),
+        in_specs=[vmem] * 6,
+        out_specs=vmem,
+        scratch_shapes=[
+            pltpu.VMEM((slots, local), jnp.int32),
+            pltpu.VMEM((slots, local), f32),
+            pltpu.VMEM((1, local), f32),
+            pltpu.VMEM((tiles, SPAN, TILE), bf16),
+            pltpu.VMEM((tiles, SPAN, TILE), bf16),
+            pltpu.VMEM((2 * vector_count, local + 2 * REACH), bf16),
+            pltpu.VMEM((vector_count, local), f32),
+            pltpu.VMEM((vector_count, local), f32),
+            pltpu.VMEM((4, vector_count, REACH), f32),
+            pltpu.VMEM((8, 8, vector_count), f32),
+            pltpu.VMEM((7, 8, vector_count), f32),
+            pltpu.VMEM((8, vector_count), f32),
+            pltpu.VMEM((planes - 1, 8, vector_count), f32),
+            pltpu.VMEM((8, vector_count), f32),
+            pltpu.VMEM((8, 8, vector_count), f32),
+            pltpu.VMEM((vector_count, local), f32),
+            pltpu.SemaphoreType.DMA((30,)),
+            pltpu.SemaphoreType.DMA((30,)),
+        ],
+        compiler_params=pltpu.CompilerParams(
+            collective_id=0, has_side_effects=True, vmem_limit_bytes=40 * 1024 * 1024
+        ),
+    )(vectors, offsets, counts.reshape(1, local), labels, cosines, distances)
+
+
+def fits(row_count, col_count, vectors):
+    vector_count, local = vectors.shape
+    return (
+        col_count == 2
+        and row_count in (8, 12, 16, 20, 24, 28, 32)
+        and vector_count == 2 * BLOCK
+        and local % TILE == 0
+        and local >= 2 * TILE
+    )
+
+
+def on_slice(row_count, col_count, *arguments):
+    if fits(row_count, col_count, arguments[0]):
+        return fused(row_count, col_count, *arguments)
+    return on_device(*arguments)
+
+
 def solution(mesh):
     placed = (
         P(None, ("rows", "cols")),
@@ -102,5 +434,6 @@
         P(None, ("rows", "cols")),
     )
     return jax.shard_map(
-        on_device, mesh=mesh, in_specs=placed, out_specs=P("cols", "rows"), check_vma=False
-    )
+        functools.partial(on_slice, mesh.shape["rows"], mesh.shape["cols"]),
+        mesh=mesh, in_specs=placed, out_specs=P("cols", "rows"), check_vma=False
+    )

time: 344 us -> 46.3 us (0.13)
  the two profiles are of different devices: /device:TPU:0 before, /device:TPU:3 now
where the time goes in v1:
time: 46.3 us; the launch traced here: 46 us
  Pallas kernels  40.2 us (87%)
  local copies, waits for them, and re-layouts  5.74 us (12%)
    pallas_call x1, Pallas kernels, fused(): pl.pallas_call(functools.partial(kernel, row_count, col_count, local * ro...  40.2 us
    unnamed x13, local copies, waits for them, and re-layouts  5.74 us

profile of v1, /device:TPU:3, one launch (start us, length us, event | category | flops | bytes accessed | tf_op | source)
XLA Modules:
  0.0 46.0 jit_solution(14668765967097266071)
XLA Ops:
  0.0 0.0 copy-start
  0.0 1.0 %copy-done = f32[128,1024]{1,0:T(8,128)S(1)} copy-done((f32[128,1024]{1,0:T(8,128)S(1)}, f32[128,1024]{1,0:T(8,128)}, u32[]{:S(2)}) %copy-start) | copy-done | bytes 524312
  1.0 0.0 copy-start.1
  1.0 0.8 %copy-done.1 = s32[16,1024]{1,0:T(8,128)S(1)} copy-done((s32[16,1024]{1,0:T(8,128)S(1)}, s32[16,1024]{1,0:T(8,128)}, u32[]{:S(2)}) %copy-start.1) | copy-done | bytes 65560
  1.9 0.0 copy-start.2
  1.9 0.8 %copy-done.2 = f32[16,1024]{1,0:T(8,128)S(1)} copy-done((f32[16,1024]{1,0:T(8,128)S(1)}, f32[16,1024]{1,0:T(8,128)}, u32[]{:S(2)}) %copy-start.2) | copy-done | bytes 65560
  2.7 0.0 copy-start.3
  2.7 0.8 %copy-done.3 = f32[16,1024]{1,0:T(8,128)S(1)} copy-done((f32[16,1024]{1,0:T(8,128)S(1)}, f32[16,1024]{1,0:T(8,128)}, u32[]{:S(2)}) %copy-start.3) | copy-done | bytes 65560
  3.6 0.0 copy-start.4
  3.6 0.7 %copy-done.4 = s32[2,1024]{1,0:T(2,128)S(1)} copy-done((s32[2,1024]{1,0:T(2,128)S(1)}, s32[2,1024]{1,0:T(2,128)}, u32[]{:S(2)}) %copy-start.4) | copy-done | bytes 8216
  4.3 0.0 copy-start.5
  4.3 0.7 %copy-done.5 = s32[1024]{0:T(1024)S(1)} copy-done((s32[1024]{0:T(1024)S(1)}, s32[1024]{0:T(1024)}, u32[]{:S(2)}) %copy-start.5) | copy-done | bytes 4120
  4.9 40.2 %shard_map.64 = f32[64,2048]{1,0:T(8,128)S(1)} custom-call(f32[128,1024]{1,0:T(8,128)S(1)} %copy-done, s32[16,1024]{1,0:T(8,128)S(1)} %copy-done.1, s32[1,1024]{1,0:T(1,128)S(1)} %bitcast.1, s32[2,1024]{1,0:T(2,128)S(1)} %copy-done.4, f32[16,1024]{1,0:T(8,128)S(1)} %copy-done.2, f32[16,1024]{1,0:T(8,128)S(1)} %copy-done.3), custom_call_target="tpu_custom_call" | custom-call | tf_op jit(solution)/shard_map/pallas_call | solution.py:379
  45.2 0.8 %copy.8 = f32[64,2048]{1,0:T(8,128)} copy(f32[64,2048]{1,0:T(8,128)S(1)} %shard_map.64) | data formatting | bytes 1048576
Async XLA Ops:
  0.0 1.0 %copy-start = (f32[128,1024]{1,0:T(8,128)S(1)}, f32[128,1024]{1,0:T(8,128)}, u32[]{:S(2)}) copy-start(f32[128,1024]{1,0:T(8,128)} %v_ref.1) | copy-start | bytes 1572868
  1.0 0.8 %copy-start.1 = (s32[16,1024]{1,0:T(8,128)S(1)}, s32[16,1024]{1,0:T(8,128)}, u32[]{:S(2)}) copy-start(s32[16,1024]{1,0:T(8,128)} %off_ref.1) | copy-start | bytes 196612
  1.9 0.8 %copy-start.2 = (f32[16,1024]{1,0:T(8,128)S(1)}, f32[16,1024]{1,0:T(8,128)}, u32[]{:S(2)}) copy-start(f32[16,1024]{1,0:T(8,128)} %cos_ref.1) | copy-start | bytes 196612
  2.7 0.8 %copy-start.3 = (f32[16,1024]{1,0:T(8,128)S(1)}, f32[16,1024]{1,0:T(8,128)}, u32[]{:S(2)}) copy-start(f32[16,1024]{1,0:T(8,128)} %dist_ref.1) | copy-start | bytes 196612
  3.6 0.7 %copy-start.4 = (s32[2,1024]{1,0:T(2,128)S(1)}, s32[2,1024]{1,0:T(2,128)}, u32[]{:S(2)}) copy-start(s32[2,1024]{1,0:T(2,128)} %lab_ref.1) | copy-start | bytes 24580
  4.3 0.7 %copy-start.5 = (s32[1024]{0:T(1024)S(1)}, s32[1024]{0:T(1024)}, u32[]{:S(2)}) copy-start(s32[1024]{0:T(1024)} %param.8) | copy-start | bytes 12292

commit v2 on v1

--- a/solution.py
+++ b/solution.py
@@ -128,27 +128,52 @@
     lanes = lax.broadcasted_iota(jnp.int32, (size, size), 1)
     eye = jnp.where(rows == lanes, 1.0, 0.0).astype(jnp.float32)
     wide = jnp.concatenate([gram, eye], axis=1)
-    parts = [wide[8 * b : 8 * b + 8, :] for b in range(size // 8)]
-    sub = lax.broadcasted_iota(jnp.int32, (8, 1), 0)
-    for k in range(size - 1):
-        b, s = k // 8, k % 8
-        row = parts[b][s : s + 1, :]
-        scaled = row * (1.0 / row[:, k : k + 1])
-        for i in range(b, size // 8):
-            column = parts[i][:, k : k + 1]
-            if i == b:
-                column = jnp.where(sub > s, column, 0.0)
-            parts[i] = parts[i] - column * scaled
-    done = jnp.concatenate(parts, axis=0)
-    pivots = jnp.sum(jnp.where(rows == lanes, done[:, :size], 0.0), axis=1, keepdims=True)
-    return done[:, size:] / jnp.sqrt(pivots)
+    width = 2 * size
+    count = size // 8
+    parts = [wide[8 * b : 8 * b + 8, :] for b in range(count)]
+    sub = lax.broadcasted_iota(jnp.int32, (8, width), 0)
+
+    def lift(value, s):
+        return jnp.broadcast_to(value[s : s + 1, :], (8, width))
+
+    scales = []
+    for b in range(count):
+        columns = {
+            i: [
+                jnp.broadcast_to(parts[i][:, 8 * b + j : 8 * b + j + 1], (8, width))
+                for j in range(8)
+            ]
+            for i in range(b, count)
+        }
+        lead = columns[b]
+        for s in range(8):
+            pivot = lift(lead[s], s)
+            inverse = 1.0 / pivot
+            if s == 0:
+                scale = inverse
+            else:
+                scale = jnp.where(sub == s, inverse, scale)
+            factors = {i: columns[i][s] * inverse for i in range(b, count)}
+            factors[b] = jnp.where(sub > s, factors[b], 0.0)
+            for j in range(s + 1, 8):
+                top = lift(lead[j], s)
+                for i in range(b, count):
+                    columns[i][j] = columns[i][j] - factors[i] * top
+            top = lift(parts[b], s)
+            for i in range(b, count):
+                parts[i] = parts[i] - factors[i] * top
+        scales.append(scale)
+    return jnp.concatenate(
+        [(parts[b] * jnp.sqrt(scales[b]))[:, size:] for b in range(count)], axis=0
+    )
 
 
 def kernel(
     row_count, col_count, atom_total,
-    v_ref, off_ref, cnt_ref, lab_ref, cos_ref, dist_ref, out_ref,
-    key, hop, site, w_high, w_low, ext, mid, fin, halo, gram, rs, slab, zs, tot, gat, swap,
-    send, recv,
+    v_hbm, off_hbm, cnt_hbm, lab_hbm, cos_hbm, dist_hbm, out_ref,
+    v_ref, off_ref, cnt_ref, lab_ref, cos_ref, dist_ref,
+    key, hop, site, w_high, w_low, ext, ext_2, mid, fin, halo, gram, rs, slab, zs, tot, gat, swap,
+    send, recv, load,
 ):
     vector_count, local = v_ref.shape
     tiles = local // TILE
@@ -162,16 +187,28 @@
     left = (behind // col_count, lax.rem(behind, col_count))
     bit0, bit1 = lax.rem(r, 2), lax.rem(r // 2, 2)
     z = r // 4
-    mine = c + 2 * lax.rem(r, 4)
+    mine = lax.rem(r, 4)
+
+    loads = [
+        pltpu.make_async_copy(source, target, load.at[n])
+        for n, (source, target) in enumerate((
+            (off_hbm, off_ref), (cos_hbm, cos_ref), (dist_hbm, dist_ref),
+            (cnt_hbm, cnt_ref), (lab_hbm, lab_ref), (v_hbm, v_ref),
+        ))
+    ]
+    for copy in loads:
+        copy.start()
 
     group = []
-    for j in range(1, 8):
-        pc = 1 - c if j & 1 else c
-        p0 = 1 - bit0 if j & 2 else bit0
-        p1 = 1 - bit1 if j & 4 else bit1
-        group.append(((4 * z + 2 * p1 + p0, pc), pc + 2 * p0 + 4 * p1))
+    for j in range(1, 4):
+        p0 = 1 - bit0 if j & 1 else bit0
+        p1 = 1 - bit1 if j & 2 else bit1
+        group.append(((4 * z + 2 * p1 + p0, c), p0 + 2 * p1))
     peers = [
-        (4 * lax.rem(z + d, planes) + lax.rem(r, 4), c) for d in range(1, planes)
+        (4 * lax.rem(z + d, planes) + lax.rem(r, 4), 1 - c if dx else c)
+        for dx in range(2)
+        for d in range(planes)
+        if dx or d
     ]
 
     barrier = pltpu.get_barrier_semaphore()
@@ -195,8 +232,10 @@
         to_left.start()
         return to_right, to_left
 
-    halo_a = edges(v_ref, 0)
-
+    halo_a = edges(v_hbm, 0)
+
+    for copy in loads[:5]:
+        copy.wait()
     lane = lax.broadcasted_iota(jnp.int32, (1, local), 1)
     key[...] = off_ref[...] + (lax.rem(lane, HALF) + REACH)
     hop[...] = hop_table_2(cos_ref[...], dist_ref[...], cnt_ref[...])
@@ -204,18 +243,16 @@
     signs = (2 * lab - 1).astype(jnp.float32)
     site[...] = SITE_MASS * signs[0:1, :] + LAYER_BIAS * signs[1:2, :]
 
-    def put_ext(value, first, width):
+    def put_ext(target, value, first, width):
         high, low = split_2(value)
-        ext[0:vector_count, first : first + width] = high
-        ext[vector_count : 2 * vector_count, first : first + width] = low
-
-    put_ext(v_ref[...], REACH, local)
+        target[0:vector_count, first : first + width] = high
+        target[vector_count : 2 * vector_count, first : first + width] = low
 
     slots = off_ref.shape[0]
     chunk = 32
     row8 = lax.broadcasted_iota(jnp.int32, (8, HALF), 0)
 
-    def build(t, carry):
+    def build(t):
         for half in range(2):
             lanes = pl.ds(pl.multiple_of(t * TILE + half * HALF, HALF), HALF)
             keys = key[:, lanes]
@@ -243,11 +280,18 @@
             edge = pl.ds(BAND if half == 0 else 0, HALF)
             w_high[t, edge, pl.ds(half * HALF, HALF)] = blank
             w_low[t, edge, pl.ds(half * HALF, HALF)] = blank
+
+    def build_edge(n, carry):
+        build(n * (tiles - 1))
         return carry
 
-    lax.fori_loop(0, tiles, build, 0)
-
-    def apply(t, source, target):
+    def build_inner(n, carry):
+        build(n)
+        return carry
+
+    lax.fori_loop(0, 2, build_edge, 0)
+
+    def apply(t, ext, source, target):
         lanes = slice(t * TILE, (t + 1) * TILE)
         span = slice(t * TILE, t * TILE + SPAN)
         both = dot_nn(ext[:, span], w_high[t])
@@ -255,21 +299,50 @@
         value = value + dot_nn(ext[0:vector_count, span], w_low[t])
         target[:, lanes] = value + site[:, lanes] * source[:, lanes]
 
-    def finish(source, target, arrivals, first):
-        to_right, to_left = arrivals
-        for t in range(1, tiles - 1):
-            apply(t, source, target)
-        to_right.wait_recv()
-        put_ext(halo[first], 0, REACH)
-        apply(0, source, target)
-        to_left.wait_recv()
-        put_ext(halo[first + 1], REACH + local, REACH)
-        apply(tiles - 1, source, target)
-
-    finish(v_ref, mid, halo_a, 0)
+    last = tiles - 1
+    loads[5].wait()
+    put_ext(ext, v_ref[...], REACH, local)
+    halo_a[0].wait_recv()
+    halo_a[1].wait_recv()
+    put_ext(ext, halo[0], 0, REACH)
+    put_ext(ext, halo[1], REACH + local, REACH)
+    apply(0, ext, v_ref, mid)
+    apply(last, ext, v_ref, mid)
     halo_b = edges(mid, 2)
-    put_ext(mid[...], REACH, local)
-    finish(mid, fin, halo_b, 2)
+
+    lax.fori_loop(1, last, build_inner, 0)
+    for t in range(1, last):
+        apply(t, ext, v_ref, mid)
+    put_ext(ext_2, mid[...], REACH, local)
+
+    partner = (r, 1 - c)
+    base = 20
+    swaps = []
+
+    def send_tile(t):
+        pair = []
+        for b in range(2):
+            piece = (pl.ds(b * BLOCK, BLOCK), pl.ds(t * TILE, TILE))
+            pair.append(
+                remote(base + 2 * t + b, fin.at[piece], swap.at[piece], partner)
+            )
+        pair[0].start()
+
+        @pl.when(c == 0)
+        def _():
+            pair[1].start()
+
+        swaps.append((t, pair))
+
+    for t in range(1, last):
+        apply(t, ext_2, mid, fin)
+        send_tile(t)
+    halo_b[0].wait_recv()
+    halo_b[1].wait_recv()
+    put_ext(ext_2, halo[2], 0, REACH)
+    put_ext(ext_2, halo[3], REACH + local, REACH)
+    apply(0, ext_2, mid, fin)
+    apply(last, ext_2, mid, fin)
 
     high, low = split_2(fin[...])
     lead = jnp.concatenate([high[0:BLOCK], low[0:BLOCK]], axis=0)
@@ -278,51 +351,44 @@
         pair[BLOCK:, 0:vector_count] + pair[0:BLOCK, vector_count:]
     )
     part = part * (1.0 / atom_total)
-    for b in range(8):
-        gram[b] = part[8 * b : 8 * b + 8, :]
-
-    first = 4
+    for b in range(4):
+        gram[b] = part[16 * b : 16 * b + 16, :]
+
     scatter = []
-    for j in range(7):
+    for j in range(3):
         device, index = group[j]
-        copy = remote(first + j, gram.at[index], rs.at[j], device)
+        copy = remote(4 + j, gram.at[index], rs.at[j], device)
         copy.start()
         scatter.append(copy)
-
-    partner = (r, 1 - c)
-    swap_a = remote(28, fin.at[pl.ds(0, BLOCK)], swap.at[pl.ds(0, BLOCK)], partner)
-    swap_b = remote(29, fin.at[pl.ds(BLOCK, BLOCK)], swap.at[pl.ds(BLOCK, BLOCK)], partner)
-    swap_a.start()
-
-    @pl.when(c == 0)
-    def _():
-        swap_b.start()
+    send_tile(0)
+    send_tile(last)
 
     value = gram[mine]
-    for j in range(7):
+    for j in range(3):
         scatter[j].wait_recv()
         value = value + rs[j]
     slab[...] = value
     across = []
-    for d in range(planes - 1):
-        copy = remote(11 + d, slab, zs.at[d], peers[d])
+    first = base + 2 * tiles
+    for d in range(len(peers)):
+        copy = remote(first + d, slab, zs.at[d], peers[d])
         copy.start()
         across.append(copy)
-    for d in range(planes - 1):
+    for d in range(len(peers)):
         across[d].wait_recv()
         value = value + zs[d]
     tot[...] = value
     gather = []
-    for j in range(7):
-        copy = remote(21 + j, tot, gat.at[mine], group[j][0])
+    for j in range(3):
+        copy = remote(7 + j, tot, gat.at[mine], group[j][0])
         copy.start()
         gather.append(copy)
     gat[mine] = value
-    for j in range(7):
+    for j in range(3):
         gather[j].wait_recv()
 
     highest = lax.Precision.HIGHEST
-    full = jnp.concatenate([gat[b] for b in range(8)], axis=0)
+    full = jnp.concatenate([gat[b] for b in range(4)], axis=0)
     inverse = inverse_factor(full[:, 0:BLOCK])
     coupling = jnp.dot(
         inverse, full[:, BLOCK:], precision=highest, preferred_element_type=jnp.float32
@@ -343,22 +409,27 @@
     own = result(high[0:BLOCK], low[0:BLOCK], fin[BLOCK:, :])
     out_ref[:, pl.ds(pl.multiple_of(c * local, local), local)] = own
 
-    swap_a.wait_recv()
-
-    @pl.when(c == 1)
-    def _():
-        swap_b.wait_recv()
-
-    other_high, other_low = split_2(swap[0:BLOCK, :])
-    theirs = result(other_high, other_low, swap[BLOCK:, :])
-    out_ref[:, pl.ds(pl.multiple_of((1 - c) * local, local), local)] = theirs
-
-    for copy in (*halo_a, *halo_b, *scatter, *across, *gather, swap_a):
+    there = pl.multiple_of((1 - c) * local, local)
+    for t, pair in swaps:
+        pair[0].wait_recv()
+
+        @pl.when(c == 1)
+        def _():
+            pair[1].wait_recv()
+
+        lanes = slice(t * TILE, (t + 1) * TILE)
+        other_high, other_low = split_2(swap[0:BLOCK, lanes])
+        theirs = result(other_high, other_low, swap[BLOCK:, lanes])
+        out_ref[:, pl.ds(pl.multiple_of(there + t * TILE, TILE), TILE)] = theirs
+
+    for copy in (*halo_a, *halo_b, *scatter, *across, *gather):
         copy.wait_send()
-
-    @pl.when(c == 0)
-    def _():
-        swap_b.wait_send()
+    for t, pair in swaps:
+        pair[0].wait_send()
+
+        @pl.when(c == 0)
+        def _():
+            pair[1].wait_send()
 
 
 def hop_table_2(cosines, distances, counts):
@@ -376,33 +447,43 @@
     planes = row_count // 4
     f32, bf16 = jnp.float32, jnp.bfloat16
     vmem = pl.BlockSpec(memory_space=pltpu.VMEM)
+    peers = 2 * planes - 1
+    semaphores = 20 + 2 * tiles + peers
     return pl.pallas_call(
         functools.partial(kernel, row_count, col_count, local * row_count * col_count),
         out_shape=jax.ShapeDtypeStruct((BLOCK, local * col_count), f32),
-        in_specs=[vmem] * 6,
+        in_specs=[pl.BlockSpec(memory_space=pltpu.HBM)] * 6,
         out_specs=vmem,
         scratch_shapes=[
+            pltpu.VMEM((vector_count, local), f32),
+            pltpu.VMEM((slots, local), jnp.int32),
+            pltpu.VMEM((1, local), jnp.int32),
+            pltpu.VMEM((2, local), jnp.int32),
+            pltpu.VMEM((slots, local), f32),
+            pltpu.VMEM((slots, local), f32),
             pltpu.VMEM((slots, local), jnp.int32),
             pltpu.VMEM((slots, local), f32),
             pltpu.VMEM((1, local), f32),
             pltpu.VMEM((tiles, SPAN, TILE), bf16),
             pltpu.VMEM((tiles, SPAN, TILE), bf16),
             pltpu.VMEM((2 * vector_count, local + 2 * REACH), bf16),
+            pltpu.VMEM((2 * vector_count, local + 2 * REACH), bf16),
             pltpu.VMEM((vector_count, local), f32),
             pltpu.VMEM((vector_count, local), f32),
             pltpu.VMEM((4, vector_count, REACH), f32),
-            pltpu.VMEM((8, 8, vector_count), f32),
-            pltpu.VMEM((7, 8, vector_count), f32),
-            pltpu.VMEM((8, vector_count), f32),
-            pltpu.VMEM((planes - 1, 8, vector_count), f32),
-            pltpu.VMEM((8, vector_count), f32),
-            pltpu.VMEM((8, 8, vector_count), f32),
+            pltpu.VMEM((4, 16, vector_count), f32),
+            pltpu.VMEM((3, 16, vector_count), f32),
+            pltpu.VMEM((16, vector_count), f32),
+            pltpu.VMEM((peers, 16, vector_count), f32),
+            pltpu.VMEM((16, vector_count), f32),
+            pltpu.VMEM((4, 16, vector_count), f32),
             pltpu.VMEM((vector_count, local), f32),
-            pltpu.SemaphoreType.DMA((30,)),
-            pltpu.SemaphoreType.DMA((30,)),
+            pltpu.SemaphoreType.DMA((semaphores,)),
+            pltpu.SemaphoreType.DMA((semaphores,)),
+            pltpu.SemaphoreType.DMA((6,)),
         ],
         compiler_params=pltpu.CompilerParams(
-            collective_id=0, has_side_effects=True, vmem_limit_bytes=40 * 1024 * 1024
+            collective_id=0, has_side_effects=True, vmem_limit_bytes=60 * 1024 * 1024
         ),
     )(vectors, offsets, counts.reshape(1, local), labels, cosines, distances)
 

time: 46.3 us -> 40 us (0.86)
  the two profiles are of different devices: /device:TPU:3 before, /device:TPU:0 now
where the time goes in v2:
time: 40 us; the launch traced here: 39.8 us
  Pallas kernels  38 us (95%)
  local copies, waits for them, and re-layouts  1.87 us (5%)
    pallas_call x1, Pallas kernels, fused(): pl.pallas_call(functools.partial(kernel, row_count, col_count, local * ro...  38 us
    unnamed x1, local copies, waits for them, and re-layouts  1.87 us

profile of v2, /device:TPU:0, one launch (start us, length us, event | category | flops | bytes accessed | tf_op | source)
XLA Modules:
  0.0 39.8 jit_solution(12364389889915807286)
XLA Ops:
  0.0 38.0 %shard_map.64 = f32[64,2048]{1,0:T(8,128)} custom-call(f32[128,1024]{1,0:T(8,128)} %v_hbm.1, s32[16,1024]{1,0:T(8,128)} %off_hbm.1, s32[1,1024]{1,0:T(1,128)} %bitcast.1, s32[2,1024]{1,0:T(2,128)} %lab_hbm.1, f32[16,1024]{1,0:T(8,128)} %cos_hbm.1, f32[16,1024]{1,0:T(8,128)} %dist_hbm.1), custom_call_target="tpu_custom_call" | custom-call | tf_op jit(solution)/shard_map/pallas_call | solution.py:452
  38.0 1.9 %copy.8 = f32[64,2048]{1,0:T(8,128)} copy(f32[64,2048]{1,0:T(8,128)} %shard_map.64) | data formatting | bytes 1048576

commit v3 on v2

--- a/solution.py
+++ b/solution.py
@@ -215,7 +215,6 @@
     greeted = [left, right] + [g[0] for g in group] + peers
     for device in greeted:
         pl.semaphore_signal(barrier, inc=1, device_id=device, device_id_type=MESH)
-    pl.semaphore_wait(barrier, len(greeted))
 
     def remote(slot, source, target, device):
         return pltpu.make_async_remote_copy(
@@ -232,16 +231,21 @@
         to_left.start()
         return to_right, to_left
 
-    halo_a = edges(v_hbm, 0)
-
     for copy in loads[:5]:
         copy.wait()
     lane = lax.broadcasted_iota(jnp.int32, (1, local), 1)
-    key[...] = off_ref[...] + (lax.rem(lane, HALF) + REACH)
-    hop[...] = hop_table_2(cos_ref[...], dist_ref[...], cnt_ref[...])
+    keys_all, hops_all = merged(
+        off_ref[...] + (lax.rem(lane, HALF) + REACH),
+        hop_table_2(cos_ref[...], dist_ref[...], cnt_ref[...]),
+    )
+    key[...] = keys_all
+    hop[...] = hops_all
     lab = lab_ref[...]
     signs = (2 * lab - 1).astype(jnp.float32)
     site[...] = SITE_MASS * signs[0:1, :] + LAYER_BIAS * signs[1:2, :]
+
+    pl.semaphore_wait(barrier, len(greeted))
+    halo_a = edges(v_hbm, 0)
 
     def put_ext(target, value, first, width):
         high, low = split_2(value)
@@ -249,30 +253,34 @@
         target[vector_count : 2 * vector_count, first : first + width] = low
 
     slots = off_ref.shape[0]
-    chunk = 32
-    row8 = lax.broadcasted_iota(jnp.int32, (8, HALF), 0)
+    chunk = 64
+    row16 = lax.broadcasted_iota(jnp.int32, (16, HALF), 0)
 
     def build(t):
         for half in range(2):
             lanes = pl.ds(pl.multiple_of(t * TILE + half * HALF, HALF), HALF)
+            span = pl.ds(half * HALF, HALF)
             keys = key[:, lanes]
             hops = hop[:, lanes]
-            keys = [jnp.broadcast_to(keys[k : k + 1, :], (8, HALF)) for k in range(slots)]
-            hops = [jnp.broadcast_to(hops[k : k + 1, :], (8, HALF)) for k in range(slots)]
+            keys = [
+                jnp.broadcast_to(keys[k : k + 1, :], (16, HALF)).astype(jnp.int16)
+                for k in range(slots)
+            ]
+            hops = [
+                split_2(jnp.broadcast_to(hops[k : k + 1, :], (16, HALF))) for k in range(slots)
+            ]
 
             def rows(q, inner):
-                parts = []
-                for piece in range(chunk // 8):
-                    index = row8 + (q * chunk + piece * 8)
-                    terms = jnp.where(keys[0] == index, hops[0], 0.0)
-                    for k in range(1, slots):
-                        terms = terms + jnp.where(keys[k] == index, hops[k], 0.0)
-                    parts.append(terms)
-                high, low = split_2(jnp.concatenate(parts, axis=0))
-                where = pl.ds(pl.multiple_of(q * chunk + half * HALF, chunk), chunk)
-                span = pl.ds(half * HALF, HALF)
-                w_high[t, where, span] = high
-                w_low[t, where, span] = low
+                for piece in range(chunk // 16):
+                    index = (row16 + (q * chunk + piece * 16)).astype(jnp.int16)
+                    high = low = jnp.zeros((16, HALF), jnp.bfloat16)
+                    for k in range(slots):
+                        here = keys[k] == index
+                        high = jnp.where(here, hops[k][0], high)
+                        low = jnp.where(here, hops[k][1], low)
+                    first = pl.multiple_of(q * chunk + piece * 16 + half * HALF, 16)
+                    w_high[t, pl.ds(first, 16), span] = high
+                    w_low[t, pl.ds(first, 16), span] = low
                 return inner
 
             lax.fori_loop(0, BAND // chunk, rows, 0)
@@ -432,6 +440,21 @@
             pair[1].wait_send()
 
 
+def merged(keys, values):
+    count = keys.shape[0]
+    row = lax.broadcasted_iota(jnp.int32, keys.shape, 0)
+    repeated = jnp.zeros(keys.shape, jnp.int32)
+    total = values
+    for shift in range(1, count):
+        near = jnp.concatenate([keys[count - shift :], keys[: count - shift]], axis=0)
+        value = jnp.concatenate([values[count - shift :], values[: count - shift]], axis=0)
+        same = near == keys
+        later = row < shift
+        total = total + jnp.where(same & later, value, 0.0)
+        repeated = jnp.where(same & ~later, 1, repeated)
+    return jnp.where(repeated == 1, -1, keys), total
+
+
 def hop_table_2(cosines, distances, counts):
     square = cosines * cosines
     bond_value = PI_BOND * jnp.exp(-(distances - 1.0) / DECAY_LENGTH) * (1.0 - square)
@@ -451,7 +474,7 @@
     semaphores = 20 + 2 * tiles + peers
     return pl.pallas_call(
         functools.partial(kernel, row_count, col_count, local * row_count * col_count),
-        out_shape=jax.ShapeDtypeStruct((BLOCK, local * col_count), f32),
+        out_shape=pltpu.VMEM((BLOCK, local * col_count), f32),
         in_specs=[pl.BlockSpec(memory_space=pltpu.HBM)] * 6,
         out_specs=vmem,
         scratch_shapes=[

time: 40 us -> 38.5 us (0.963)
  local copies, waits for them, and re-layouts: 1.87 us -> 0.8 us
  Pallas kernels: 38 us -> 37.5 us
    unnamed x1, local copies, waits for them, and re-layouts: 1.87 us -> 0.8 us
    pallas_call x1, Pallas kernels: 38 us -> 37.5 us  [fused(): pl.pallas_call(functools.partial(kernel, row_count, col_count, local * ro...]
where the time goes in v3:
time: 38.5 us; the launch traced here: 38.3 us
  Pallas kernels  37.5 us (97%)
  local copies, waits for them, and re-layouts  0.8 us (2%)
    pallas_call x1, Pallas kernels, fused(): pl.pallas_call(functools.partial(kernel, row_count, col_count, local * ro...  37.5 us
    unnamed x1, local copies, waits for them, and re-layouts  0.8 us

profile of v3, /device:TPU:0, one launch (start us, length us, event | category | flops | bytes accessed | tf_op | source)
XLA Modules:
  0.0 38.3 jit_solution(3366182130437836065)
XLA Ops:
  0.0 37.5 %shard_map.64 = f32[64,2048]{1,0:T(8,128)S(1)} custom-call(f32[128,1024]{1,0:T(8,128)} %v_hbm.1, s32[16,1024]{1,0:T(8,128)} %off_hbm.1, s32[1,1024]{1,0:T(1,128)} %bitcast.1, s32[2,1024]{1,0:T(2,128)} %lab_hbm.1, f32[16,1024]{1,0:T(8,128)} %cos_hbm.1, f32[16,1024]{1,0:T(8,128)} %dist_hbm.1), custom_call_target="tpu_custom_call" | custom-call | tf_op jit(solution)/shard_map/pallas_call | solution.py:475
  37.5 0.8 %copy.8 = f32[64,2048]{1,0:T(8,128)} copy(f32[64,2048]{1,0:T(8,128)S(1)} %shard_map.64) | data formatting | bytes 1048576

commit v4 on v3

--- a/solution.py
+++ b/solution.py
@@ -172,7 +172,7 @@
     row_count, col_count, atom_total,
     v_hbm, off_hbm, cnt_hbm, lab_hbm, cos_hbm, dist_hbm, out_ref,
     v_ref, off_ref, cnt_ref, lab_ref, cos_ref, dist_ref,
-    key, hop, site, w_high, w_low, ext, ext_2, mid, fin, halo, gram, rs, slab, zs, tot, gat, swap,
+    key, hop, site, w_high, w_low, ext, ext_2, mid, fin, halo, gram, gx, gsum, rs, slab, zs, tot, gat, swap,
     send, recv, load,
 ):
     vector_count, local = v_ref.shape
@@ -204,15 +204,11 @@
         p0 = 1 - bit0 if j & 1 else bit0
         p1 = 1 - bit1 if j & 2 else bit1
         group.append(((4 * z + 2 * p1 + p0, c), p0 + 2 * p1))
-    peers = [
-        (4 * lax.rem(z + d, planes) + lax.rem(r, 4), 1 - c if dx else c)
-        for dx in range(2)
-        for d in range(planes)
-        if dx or d
-    ]
+    peers = [(4 * lax.rem(z + d, planes) + lax.rem(r, 4), c) for d in range(1, planes)]
+    partner = (r, 1 - c)
 
     barrier = pltpu.get_barrier_semaphore()
-    greeted = [left, right] + [g[0] for g in group] + peers
+    greeted = [left, right, partner] + [g[0] for g in group] + peers
     for device in greeted:
         pl.semaphore_signal(barrier, inc=1, device_id=device, device_id_type=MESH)
 
@@ -289,15 +285,11 @@
             w_high[t, edge, pl.ds(half * HALF, HALF)] = blank
             w_low[t, edge, pl.ds(half * HALF, HALF)] = blank
 
-    def build_edge(n, carry):
-        build(n * (tiles - 1))
-        return carry
-
-    def build_inner(n, carry):
+    def build_all(n, carry):
         build(n)
         return carry
 
-    lax.fori_loop(0, 2, build_edge, 0)
+    lax.fori_loop(0, tiles, build_all, 0)
 
     def apply(t, ext, source, target):
         lanes = slice(t * TILE, (t + 1) * TILE)
@@ -310,6 +302,8 @@
     last = tiles - 1
     loads[5].wait()
     put_ext(ext, v_ref[...], REACH, local)
+    for t in range(1, last):
+        apply(t, ext, v_ref, mid)
     halo_a[0].wait_recv()
     halo_a[1].wait_recv()
     put_ext(ext, halo[0], 0, REACH)
@@ -317,13 +311,8 @@
     apply(0, ext, v_ref, mid)
     apply(last, ext, v_ref, mid)
     halo_b = edges(mid, 2)
-
-    lax.fori_loop(1, last, build_inner, 0)
-    for t in range(1, last):
-        apply(t, ext, v_ref, mid)
     put_ext(ext_2, mid[...], REACH, local)
 
-    partner = (r, 1 - c)
     base = 20
     swaps = []
 
@@ -344,7 +333,6 @@
 
     for t in range(1, last):
         apply(t, ext_2, mid, fin)
-        send_tile(t)
     halo_b[0].wait_recv()
     halo_b[1].wait_recv()
     put_ext(ext_2, halo[2], 0, REACH)
@@ -362,16 +350,21 @@
     for b in range(4):
         gram[b] = part[16 * b : 16 * b + 16, :]
 
+    couple = remote(10, gram, gx, partner)
+    couple.start()
+    for t in (*range(1, last), 0, last):
+        send_tile(t)
+    couple.wait_recv()
+    gsum[...] = gram[...] + gx[...]
+
     scatter = []
     for j in range(3):
         device, index = group[j]
-        copy = remote(4 + j, gram.at[index], rs.at[j], device)
+        copy = remote(4 + j, gsum.at[index], rs.at[j], device)
         copy.start()
         scatter.append(copy)
-    send_tile(0)
-    send_tile(last)
-
-    value = gram[mine]
+
+    value = gsum[mine]
     for j in range(3):
         scatter[j].wait_recv()
         value = value + rs[j]
@@ -430,7 +423,7 @@
         theirs = result(other_high, other_low, swap[BLOCK:, lanes])
         out_ref[:, pl.ds(pl.multiple_of(there + t * TILE, TILE), TILE)] = theirs
 
-    for copy in (*halo_a, *halo_b, *scatter, *across, *gather):
+    for copy in (*halo_a, *halo_b, couple, *scatter, *across, *gather):
         copy.wait_send()
     for t, pair in swaps:
         pair[0].wait_send()
@@ -470,7 +463,7 @@
     planes = row_count // 4
     f32, bf16 = jnp.float32, jnp.bfloat16
     vmem = pl.BlockSpec(memory_space=pltpu.VMEM)
-    peers = 2 * planes - 1
+    peers = planes - 1
     semaphores = 20 + 2 * tiles + peers
     return pl.pallas_call(
         functools.partial(kernel, row_count, col_count, local * row_count * col_count),
@@ -495,6 +488,8 @@
             pltpu.VMEM((vector_count, local), f32),
             pltpu.VMEM((4, vector_count, REACH), f32),
             pltpu.VMEM((4, 16, vector_count), f32),
+            pltpu.VMEM((4, 16, vector_count), f32),
+            pltpu.VMEM((4, 16, vector_count), f32),
             pltpu.VMEM((3, 16, vector_count), f32),
             pltpu.VMEM((16, vector_count), f32),
             pltpu.VMEM((peers, 16, vector_count), f32),

time: 38.5 us -> 38.7 us (level)
  no operation moved by 1% of the time
where the time goes in v4:
time: 38.7 us; the launch traced here: 38.5 us
  Pallas kernels  37.7 us (97%)
  local copies, waits for them, and re-layouts  0.8 us (2%)
    pallas_call x1, Pallas kernels, fused(): pl.pallas_call(functools.partial(kernel, row_count, col_count, local * ro...  37.7 us
    unnamed x1, local copies, waits for them, and re-layouts  0.8 us

profile of v4, /device:TPU:0, one launch (start us, length us, event | category | flops | bytes accessed | tf_op | source)
XLA Modules:
  0.0 38.5 jit_solution(7670489993046538189)
XLA Ops:
  0.0 37.7 %shard_map.64 = f32[64,2048]{1,0:T(8,128)S(1)} custom-call(f32[128,1024]{1,0:T(8,128)} %v_hbm.1, s32[16,1024]{1,0:T(8,128)} %off_hbm.1, s32[1,1024]{1,0:T(1,128)} %bitcast.1, s32[2,1024]{1,0:T(2,128)} %lab_hbm.1, f32[16,1024]{1,0:T(8,128)} %cos_hbm.1, f32[16,1024]{1,0:T(8,128)} %dist_hbm.1), custom_call_target="tpu_custom_call" | custom-call | tf_op jit(solution)/shard_map/pallas_call | solution.py:468
  37.8 0.8 %copy.8 = f32[64,2048]{1,0:T(8,128)} copy(f32[64,2048]{1,0:T(8,128)S(1)} %shard_map.64) | data formatting | bytes 1048576

commit v5 on v3

--- a/solution.py
+++ b/solution.py
@@ -148,7 +148,8 @@
         lead = columns[b]
         for s in range(8):
             pivot = lift(lead[s], s)
-            inverse = 1.0 / pivot
+            rough = pl.reciprocal(pivot, approx=True)
+            inverse = rough * (2.0 - pivot * rough)
             if s == 0:
                 scale = inverse
             else:
@@ -210,6 +211,7 @@
         for d in range(planes)
         if dx or d
     ]
+    partner = (r, 1 - c)
 
     barrier = pltpu.get_barrier_semaphore()
     greeted = [left, right] + [g[0] for g in group] + peers
@@ -289,15 +291,11 @@
             w_high[t, edge, pl.ds(half * HALF, HALF)] = blank
             w_low[t, edge, pl.ds(half * HALF, HALF)] = blank
 
-    def build_edge(n, carry):
-        build(n * (tiles - 1))
-        return carry
-
-    def build_inner(n, carry):
+    def build_all(n, carry):
         build(n)
         return carry
 
-    lax.fori_loop(0, 2, build_edge, 0)
+    lax.fori_loop(0, tiles, build_all, 0)
 
     def apply(t, ext, source, target):
         lanes = slice(t * TILE, (t + 1) * TILE)
@@ -310,6 +308,8 @@
     last = tiles - 1
     loads[5].wait()
     put_ext(ext, v_ref[...], REACH, local)
+    for t in range(1, last):
+        apply(t, ext, v_ref, mid)
     halo_a[0].wait_recv()
     halo_a[1].wait_recv()
     put_ext(ext, halo[0], 0, REACH)
@@ -317,13 +317,8 @@
     apply(0, ext, v_ref, mid)
     apply(last, ext, v_ref, mid)
     halo_b = edges(mid, 2)
-
-    lax.fori_loop(1, last, build_inner, 0)
-    for t in range(1, last):
-        apply(t, ext, v_ref, mid)
     put_ext(ext_2, mid[...], REACH, local)
 
-    partner = (r, 1 - c)
     base = 20
     swaps = []
 
@@ -344,7 +339,6 @@
 
     for t in range(1, last):
         apply(t, ext_2, mid, fin)
-        send_tile(t)
     halo_b[0].wait_recv()
     halo_b[1].wait_recv()
     put_ext(ext_2, halo[2], 0, REACH)
@@ -368,8 +362,6 @@
         copy = remote(4 + j, gram.at[index], rs.at[j], device)
         copy.start()
         scatter.append(copy)
-    send_tile(0)
-    send_tile(last)
 
     value = gram[mine]
     for j in range(3):
@@ -382,6 +374,8 @@
         copy = remote(first + d, slab, zs.at[d], peers[d])
         copy.start()
         across.append(copy)
+    for t in (*range(1, last), 0, last):
+        send_tile(t)
     for d in range(len(peers)):
         across[d].wait_recv()
         value = value + zs[d]

time: 38.5 us -> 38.6 us (level)
  the two profiles are of different devices: /device:TPU:0 before, /device:TPU:6 now
where the time goes in v5:
time: 38.6 us; the launch traced here: 38.5 us
  Pallas kernels  37.7 us (98%)
  local copies, waits for them, and re-layouts  0.8 us (2%)
    pallas_call x1, Pallas kernels, fused(): pl.pallas_call(functools.partial(kernel, row_count, col_count, local * ro...  37.7 us
    unnamed x1, local copies, waits for them, and re-layouts  0.8 us

profile of v5, /device:TPU:6, one launch (start us, length us, event | category | flops | bytes accessed | tf_op | source)
XLA Modules:
  0.0 38.5 jit_solution(435253680782353696)
XLA Ops:
  0.0 37.7 %shard_map.64 = f32[64,2048]{1,0:T(8,128)S(1)} custom-call(f32[128,1024]{1,0:T(8,128)} %v_hbm.1, s32[16,1024]{1,0:T(8,128)} %off_hbm.1, s32[1,1024]{1,0:T(1,128)} %bitcast.1, s32[2,1024]{1,0:T(2,128)} %lab_hbm.1, f32[16,1024]{1,0:T(8,128)} %cos_hbm.1, f32[16,1024]{1,0:T(8,128)} %dist_hbm.1), custom_call_target="tpu_custom_call" | custom-call | tf_op jit(solution)/shard_map/pallas_call | solution.py:469
  37.7 0.8 %copy.8 = f32[64,2048]{1,0:T(8,128)} copy(f32[64,2048]{1,0:T(8,128)S(1)} %shard_map.64) | data formatting | bytes 1048576
